TPU v7x, 512 devices: a whole 4x4x16 slice. The times are simulated.
512 devices in a mesh: geo: 64 (over z, y), cell: 8 (over x, core).
Axes of the slice: x: 4, y: 4, z: 16, core: 2. Of those that a mesh axis runs over, the one named last changes fastest.
Arguments:
- detail_rows: float32 [8192, 2048], P('geo', 'cell'), may hold values from -60 to 60
- row_block: int32 [8192], P('geo'), may hold values from 0 to 8191, as said below
- block_weight: int32 [8192], P('geo'), may hold values from 1 to 9
- block_group: int32 [8192], P('geo'), may hold values from 0 to 63, as said below
- query_matrix: int32 [2048, 512], P('cell'), may hold values 0 or 1
- query_weight: float32 [512], replicated, may hold values from 0.0048828125 to 0.048828125
- query_noisy: float32 [8192, 512], P('geo'), may hold values from -48 to 48
- group_noisy: float32 [64, 2048], P(None, 'cell'), may hold values from -48 to 48
Outputs:
- solution_field: float32 [8192, 2048], P('geo', 'cell')
- residual: float32 [8192, 2048], P('geo', 'cell')
Inputs may be any that keep to these rules, and one draw needn't show every extreme that they name: row_block is a permutation of all blocks; arrival row r lies on geo index r // 128 and its block lies on geo index (r mod 128) // 2, so each geo index sends 2 rows to each geo index. `block_group`: every group holds exactly 128 blocks.
All inputs are finite; a program needn't handle non-finite values. No bound on the sum of `query_matrix` on one device may be relied on, other than what follows from the above.
Results may differ from a plain program's by a relative error of at most 0.0029.
Values sent between devices are 32-bit elements; how exact they have to be, the bound alone decides.
A program may use at most 64 MiB of HBM per device.

v0:
```python
import jax
import jax.numpy as jnp
from jax import lax
from jax.sharding import PartitionSpec as P

QUERIES = 512
ITERS = 2
BLK_DEV = 128
AGG_WEIGHT = 0.25
HIGHEST_PREC = lax.Precision.HIGHEST
LEADING_DIMS = (((0,), (1,)), ((), ()))


def local(
    detail_rows,
    row_block,
    block_weight,
    block_group,
    query_matrix,
    query_weight,
    query_noisy,
    group_noisy,
):
    geo_index = lax.axis_index("geo")
    sent_ids = row_block.astype(jnp.float32)
    rows_in, ids_in = (
        lax.all_to_all(detail_rows, "geo", split_axis=0, concat_axis=0, tiled=True),
        lax.all_to_all(sent_ids, "geo", split_axis=0, concat_axis=0, tiled=True),
    )
    local_rows = ids_in.astype(jnp.int32) - geo_index * BLK_DEV
    detail = jnp.zeros(detail_rows.shape, jnp.float32).at[local_rows].set(rows_in)
    weight = block_weight.astype(jnp.float32)[:, None]
    queries = query_matrix.astype(jnp.float32)
    group_count = group_noisy.shape[0]
    share_rows = QUERIES // lax.axis_size("cell")

    def squares(vector):
        return lax.psum(jnp.sum(vector * vector), ("geo", "cell"))

    right_side = weight * detail
    right_side = right_side + jnp.dot(
        query_noisy * query_weight[None, :],
        queries.T,
        precision=HIGHEST_PREC,
        preferred_element_type=jnp.float32,
    )
    right_side = right_side + AGG_WEIGHT * group_noisy[block_group]
    solution_field = jnp.zeros_like(right_side)
    residual = right_side
    direction = right_side
    norm_now = squares(residual)
    for iteration in range(ITERS):
        partial_totals = jax.ops.segment_sum(direction, block_group, num_segments=group_count)
        totals = lax.psum(partial_totals, "geo")
        estimate = direction
        share_part = lax.psum_scatter(
            lax.dot_general(
                queries,
                estimate,
                LEADING_DIMS,
                precision=HIGHEST_PREC,
                preferred_element_type=jnp.float32,
            ),
            "cell",
            scatter_dimension=0,
            tiled=True,
        )
        scales = lax.dynamic_slice_in_dim(
            query_weight, lax.axis_index("cell") * share_rows, share_rows, 0
        )
        share_part = share_part * scales[:, None]
        spread_back = lax.dot_general(
            lax.all_gather(share_part, "cell", axis=0, tiled=True),
            queries,
            LEADING_DIMS,
            precision=HIGHEST_PREC,
            preferred_element_type=jnp.float32,
        )
        image_vec = weight * direction + spread_back + AGG_WEIGHT * totals[block_group]
        step_size = norm_now / lax.psum(jnp.sum(direction * image_vec), ("geo", "cell"))
        solution_field = solution_field + step_size * direction
        residual = residual - step_size * image_vec
        norm_next = squares(residual)
        direction = residual + norm_next / norm_now * direction
        norm_now = norm_next
    return (solution_field, residual)


def solution(mesh):
    return jax.shard_map(
        local,
        mesh=mesh,
        in_specs=(
            P("geo", "cell"),
            P("geo"),
            P("geo"),
            P("geo"),
            P("cell", None),
            P(),
            P("geo", None),
            P(None, "cell"),
        ),
        out_specs=(P("geo", "cell"), P("geo", "cell")),
        check_vma=False,
    )
```

profile of v0, /device:TPU:1, one launch (start us, length us, event | category | flops | bytes accessed | tf_op | source)
XLA Modules:
  0.0 915.7 jit_solution(15356650263555236824)
XLA Ops:
  8.0 0.7 convert_element_type.21
  8.7 0.8 all_to_all.14
  9.5 19.3 %all-to-all-start = ((f32[64,2,1]{1,2,0:T(1,128)}), f32[64,2,1]{1,2,0:T(1,128)S(1)}, u32[]{:S(2)}, u32[]{:S(2)}) async-start(f32[64,2,1]{1,2,0:T(1,128)} %bitcast), calls=%async_computation | async-start | bytes 65536 | tf_op jit(solution)/shard_map/all_to_all | solution.py:28
  28.7 1.6 all_to_all.16
  30.4 11.7 %all-to-all-done = f32[64,2,1]{1,2,0:T(1,128)S(1)} async-done(((f32[64,2,1]{1,2,0:T(1,128)}), f32[64,2,1]{1,2,0:T(1,128)S(1)}, u32[]{:S(2)}, u32[]{:S(2)}) %all-to-all-start) | async-done | bytes 544 | tf_op jit(solution)/shard_map/all_to_all | solution.py:28
  42.1 4.6 all-to-all-start.1
  46.8 0.6 copy-done.4
  47.5 0.8 gather_fusion
  48.6 13.3 %all-to-all-done.1 = f32[64,2,256]{2,1,0:T(2,128)S(1)} async-done(((f32[64,2,256]{2,1,0:T(2,128)}), f32[64,2,256]{2,1,0:T(2,128)S(1)}, u32[]{:S(2)}, u32[]{:S(2)}) %all-to-all-start.1) | async-done | bytes 131104 | tf_op jit(solution)/shard_map/all_to_all | solution.py:27
  62.0 1.0 scatter_custom_fusion
  63.1 0.7 fusion.2
  63.8 1.8 scatter_custom_fusion.1
  65.7 0.4 convolution_bitcast_fusion.1
  66.1 0.8 copy.16
  67.1 238.7 %all-reduce.4.cloned.1.call-done = f32[64,256]{1,0:T(8,128)} async-done(((f32[64,256]{1,0:T(8,128)}), f32[64,256]{1,0:T(8,128)}) %all-reduce.4.cloned.1.call-update) | async-done | bytes 65552 | tf_op jit(solution)/shard_map/psum | solution.py:54
  305.8 1.6 gather_fusion.1
  307.4 0.8 broadcast_multiply_fusion.1
  308.3 23.9 %all_gather.6 = f32[512,128]{1,0:T(8,128)S(1)} all-gather(f32[64,128]{1,0:T(8,128)S(1)} %broadcast_multiply_fusion.1), channel_id=1, replica_groups=mesh['geo'=64,'cell'=8] {'cell'}, dimensions={0}, use_global_device_ids=true | all-gather | bytes 294912 | tf_op jit(solution)/shard_map/all_gather | solution.py:73
  332.2 1.2 multiply_reduce_fusion.2
  333.4 100.5 %all-reduce = (f32[]{:T(128)}, f32[]{:T(128)}) all-reduce(f32[]{:T(128)} %get-tuple-element.3, f32[]{:T(128)} %get-tuple-element.2), channel_id=1, replica_groups=mesh['geo'=64,'cell'=8] {'geo','cell'}, use_global_device_ids=true, to_apply=%region_2.0 | all-reduce | flops 2 | bytes 16 | tf_op jit(solution)/shard_map/psum | solution.py:38
  435.2 0.6 multiply_reduce_fusion.1
  435.8 99.4 %psum.45 = f32[]{:T(128)} all-reduce(f32[]{:T(128)} %multiply_reduce_fusion.1), channel_id=1, replica_groups=mesh['geo'=64,'cell'=8] {'geo','cell'}, use_global_device_ids=true, to_apply=%region_9.0 | all-reduce | flops 1 | bytes 8 | tf_op jit(solution)/shard_map/psum | solution.py:38
  536.6 1.8 scatter_custom_fusion.2
  538.5 0.4 convolution_bitcast_fusion
  538.9 0.8 copy.18
  539.8 238.5 %all-reduce.6.cloned.1.call-done = f32[64,256]{1,0:T(8,128)} async-done(((f32[64,256]{1,0:T(8,128)}), f32[64,256]{1,0:T(8,128)}) %all-reduce.6.cloned.1.call-update) | async-done | bytes 65552 | tf_op jit(solution)/shard_map/psum | solution.py:54
  778.3 1.6 gather_fusion.2
  779.9 0.8 broadcast_multiply_fusion
  780.7 23.9 %all_gather.7 = f32[512,128]{1,0:T(8,128)S(1)} all-gather(f32[64,128]{1,0:T(8,128)S(1)} %broadcast_multiply_fusion), channel_id=1, replica_groups=mesh['geo'=64,'cell'=8] {'cell'}, dimensions={0}, use_global_device_ids=true | all-gather | bytes 294912 | tf_op jit(solution)/shard_map/all_gather | solution.py:73
  804.6 1.2 multiply_reduce_fusion
  805.8 100.4 %psum.47 = f32[]{:T(128)} all-reduce(f32[]{:T(128)} %get-tuple-element.9), channel_id=1, replica_groups=mesh['geo'=64,'cell'=8] {'geo','cell'}, use_global_device_ids=true, to_apply=%region_14.0 | all-reduce | flops 1 | bytes 8 | tf_op jit(solution)/shard_map/psum | solution.py:80
  907.5 0.7 multiply_subtract_fusion
  (30 shorter events, 0.8 us)
Async XLA Ops:
  8.0 39.5 %copy-start = (f32[64,256]{1,0:T(8,128)S(1)}, f32[64,256]{1,0:T(8,128)}, u32[]{:S(2)}) copy-start(f32[64,256]{1,0:T(8,128)} %param.15) | copy-start | bytes 196612
  9.5 32.7 %all-to-all-start = ((f32[64,2,1]{1,2,0:T(1,128)}), f32[64,2,1]{1,2,0:T(1,128)S(1)}, u32[]{:S(2)}, u32[]{:S(2)}) async-start(f32[64,2,1]{1,2,0:T(1,128)} %bitcast), calls=%async_computation | async-start | bytes 65536 | tf_op jit(solution)/shard_map/all_to_all | solution.py:28
  30.4 16.4 %copy-start.5 = (s32[128]{0:T(128)S(1)}, s32[128]{0:T(128)}, u32[]{:S(2)}) copy-start(s32[128]{0:T(128)} %param.11) | copy-start | bytes 1540
  42.1 19.8 %all-to-all-start.1 = ((f32[64,2,256]{2,1,0:T(2,128)}), f32[64,2,256]{2,1,0:T(2,128)S(1)}, u32[]{:S(2)}, u32[]{:S(2)}) async-start(f32[64,2,256]{2,1,0:T(2,128)} %all_to_all.16), calls=%async_computation.1 | async-start | bytes 262144 | tf_op jit(solution)/shard_map/all_to_all | solution.py:27
  46.8 259.0 %all-reduce.4.cloned.1.call-start = ((), (), s32[]{:S(2)}) async-start(), calls=%async_computation.4 | async-start | bytes 131072 | tf_op jit(solution)/shard_map/psum | solution.py:54
  46.8 0.7 copy-start.4
  47.5 15.6 %copy-start.1 = (s32[256,512]{1,0:T(8,128)S(1)}, s32[256,512]{1,0:T(8,128)}, u32[]{:S(2)}) copy-start(s32[256,512]{1,0:T(8,128)} %param.12) | copy-start | bytes 1572868
  48.3 14.8 %copy-start.2 = (f32[128,512]{1,0:T(8,128)S(1)}, f32[128,512]{1,0:T(8,128)}, u32[]{:S(2)}) copy-start(f32[128,512]{1,0:T(8,128)} %param.14) | copy-start | bytes 786436
  62.0 1.1 copy-start.3
  65.6 241.8 %reduce-scatter.7.cloned.1.call-start = ((), (), s32[]{:S(2)}) async-start(), calls=%async_computation.6 | async-start | bytes 294912 | tf_op jit(solution)/shard_map/reduce_scatter | solution.py:56
  67.0 711.3 %all-reduce.6.cloned.1.call-start = ((), (), s32[]{:S(2)}) async-start(), calls=%async_computation.5 | async-start | bytes 131072 | tf_op jit(solution)/shard_map/psum | solution.py:54
  538.4 241.5 %reduce-scatter.9.cloned.1.call-start = ((), (), s32[]{:S(2)}) async-start(), calls=%async_computation.7 | async-start | bytes 294912 | tf_op jit(solution)/shard_map/reduce_scatter | solution.py:56
Sparse Core Ops, SparseCore 0:
  65.8 239.9 all-reduce.3
  538.5 239.6 all-reduce.5
Sparse Core Ops, SparseCore 1:
  68.9 29.8 reduce-scatter.6
  541.9 28.9 reduce-scatter.8
where the time goes:
time: 917 us; the launch traced here: 916 us
  waiting for transfers between devices  502 us (55%)
  blocking collectives  348 us (38%)
  starting transfers between devices  24.1 us (3%)
  between operations  19.7 us (2%)
  local copies, waits for them, and re-layouts  10 us (1%)
    psum x2, waiting for transfers between devices, local(): totals = lax.psum(partial_totals, 'geo')  477 us
    psum x2, blocking collectives, squares(): return lax.psum(jnp.sum(vector * vector), ('geo', 'cell'))  200 us
    psum x1, blocking collectives, local(): lax.psum(jnp.sum(direction * image_vec), ('geo', 'cell'))  100 us
    all_gather x2, blocking collectives, local(): lax.all_gather(share_part, 'cell', axis=0, tiled=True)  47.8 us
    all_to_all x1, starting transfers between devices, local(): lax.all_to_all(sent_ids, 'geo', split_axis=0, concat_axis=0, tiled=True)  19.3 us
  transfers between devices with their start and end apart: 6, of which 4 were waited for; matrix products, arithmetic and copies ran while one was open for 1% of the time, Pallas kernels for 0%

commit v1 on v0

--- a/solution.py
+++ b/solution.py
@@ -9,6 +9,18 @@
 AGG_WEIGHT = 0.25
 HIGHEST_PREC = lax.Precision.HIGHEST
 LEADING_DIMS = (((0,), (1,)), ((), ()))
+
+
+def gather_by_bits(x, axis, dim):
+    ways, here = (lax.axis_size(axis), lax.axis_index(axis))
+    grown, reach = (x, 1)
+    while reach < ways:
+        theirs = lax.ppermute(grown, axis, [(d, d ^ reach) for d in range(ways)])
+        mine_first = jnp.concatenate([grown, theirs], axis=dim)
+        theirs_first = jnp.concatenate([theirs, grown], axis=dim)
+        grown = jnp.where(here & reach == 0, mine_first, theirs_first)
+        reach = 2 * reach
+    return grown
 
 
 def local(
@@ -70,7 +82,7 @@
         )
         share_part = share_part * scales[:, None]
         spread_back = lax.dot_general(
-            lax.all_gather(share_part, "cell", axis=0, tiled=True),
+            gather_by_bits(share_part, "cell", 0),
             queries,
             LEADING_DIMS,
             precision=HIGHEST_PREC,

time: 917 us -> 994 us (1.084)
  waiting for transfers between devices: 502 us -> 587 us
  blocking collectives: 348 us -> 322 us
  starting transfers between devices: 24.1 us -> 43.5 us
    unnamed x4 -> x6, waiting for transfers between devices: 0.07 us -> 58.2 us
    all_gather x2 -> x0, blocking collectives: 47.8 us -> none  [local(): lax.all_gather(share_part, 'cell', axis=0, tiled=True)]
    ppermute x0 -> x6, starting transfers between devices: none -> 19.4 us  [gather_by_bits(): theirs = lax.ppermute(grown, axis, [(d, d ^ reach) for d in range(ways)])]
    psum x2, waiting for transfers between devices: 477 us -> 495 us  [local(): totals = lax.psum(partial_totals, 'geo')]
    psum x1, blocking collectives: 100 us -> 111 us  [local(): lax.psum(jnp.sum(direction * image_vec), ('geo', 'cell'))]
    psum x2, blocking collectives: 200 us -> 211 us  [squares(): return lax.psum(jnp.sum(vector * vector), ('geo', 'cell'))]
  transfers between devices with their start and end apart: 6 -> 12, of which waited for: 4 -> 10; matrix products, arithmetic and copies ran while one was open for 1% -> 1% of each run, Pallas kernels for 0% -> 0%
where the time goes in v1:
time: 994 us; the launch traced here: 993 us
  waiting for transfers between devices  587 us (59%)
  blocking collectives  322 us (32%)
  starting transfers between devices  43.5 us (4%)
  between operations  19.6 us (2%)
  local copies, waits for them, and re-layouts  11.7 us (1%)
    psum x2, waiting for transfers between devices, local(): totals = lax.psum(partial_totals, 'geo')  495 us
    psum x2, blocking collectives, squares(): return lax.psum(jnp.sum(vector * vector), ('geo', 'cell'))  211 us
    psum x1, blocking collectives, local(): lax.psum(jnp.sum(direction * image_vec), ('geo', 'cell'))  111 us
    unnamed x6, waiting for transfers between devices  58.2 us
  transfers between devices with their start and end apart: 12, of which 10 were waited for; matrix products, arithmetic and copies ran while one was open for 1% of the time, Pallas kernels for 0%

profile of v1, /device:TPU:1, one launch (start us, length us, event | category | flops | bytes accessed | tf_op | source)
XLA Modules:
  0.0 993.4 jit_solution(7356428997880963449)
XLA Ops:
  9.5 19.3 %all-to-all-start = ((f32[64,2,1]{1,2,0:T(1,128)}), f32[64,2,1]{1,2,0:T(1,128)S(1)}, u32[]{:S(2)}, u32[]{:S(2)}) async-start(f32[64,2,1]{1,2,0:T(1,128)} %bitcast), calls=%async_computation | async-start | bytes 65536 | tf_op jit(solution)/shard_map/all_to_all | solution.py:40
  28.7 1.6 all_to_all.16
  30.4 11.7 %all-to-all-done = f32[64,2,1]{1,2,0:T(1,128)S(1)} async-done(((f32[64,2,1]{1,2,0:T(1,128)}), f32[64,2,1]{1,2,0:T(1,128)S(1)}, u32[]{:S(2)}, u32[]{:S(2)}) %all-to-all-start) | async-done | bytes 544 | tf_op jit(solution)/shard_map/all_to_all | solution.py:40
  42.1 4.6 all-to-all-start.1
  48.6 13.3 %all-to-all-done.1 = f32[64,2,256]{2,1,0:T(2,128)S(1)} async-done(((f32[64,2,256]{2,1,0:T(2,128)}), f32[64,2,256]{2,1,0:T(2,128)S(1)}, u32[]{:S(2)}, u32[]{:S(2)}) %all-to-all-start.1) | async-done | bytes 131104 | tf_op jit(solution)/shard_map/all_to_all | solution.py:39
  62.0 1.0 scatter_custom_fusion
  65.2 29.3 %reduce-scatter.7.cloned.1.call-done = f32[64,128]{1,0:T(8,128)} async-done(((f32[512,128]{1,0:T(8,128)}), f32[64,128]{1,0:T(8,128)}) %reduce-scatter.7.cloned.1.call-update) | async-done | bytes 32784
  94.5 0.8 copy.12
  95.3 4.1 collective-permute-start
  99.5 0.9 collective-permute-done
  100.4 1.9 collective-permute-start.1
  102.4 3.1 collective-permute-done.1
  105.5 3.7 collective-permute-start.2
  109.2 1.8 scatter_custom_fusion.1
  111.1 247.6 %all-reduce.4.cloned.1.call-done = f32[64,256]{1,0:T(8,128)} async-done(((f32[64,256]{1,0:T(8,128)}), f32[64,256]{1,0:T(8,128)}) %all-reduce.4.cloned.1.call-update) | async-done | bytes 65552 | tf_op jit(solution)/shard_map/psum | solution.py:66
  358.7 1.6 gather_fusion.1
  360.3 1.3 multiply_reduce_fusion.2
  361.6 111.2 %all-reduce = (f32[]{:T(128)}, f32[]{:T(128)}) all-reduce(f32[]{:T(128)} %get-tuple-element.3, f32[]{:T(128)} %get-tuple-element.2), channel_id=1, replica_groups=mesh['geo'=64,'cell'=8] {'geo','cell'}, use_global_device_ids=true, to_apply=%region_2.0 | all-reduce | flops 2 | bytes 16 | tf_op jit(solution)/shard_map/psum | solution.py:50
  474.8 99.3 %psum.45 = f32[]{:T(128)} all-reduce(f32[]{:T(128)} %multiply_reduce_fusion.1), channel_id=1, replica_groups=mesh['geo'=64,'cell'=8] {'geo','cell'}, use_global_device_ids=true, to_apply=%region_9.10 | all-reduce | flops 1 | bytes 8 | tf_op jit(solution)/shard_map/psum | solution.py:50
  575.8 0.8 copy.13
  576.7 28.9 %reduce-scatter.9.cloned.1.call-done = f32[64,128]{1,0:T(8,128)} async-done(((f32[512,128]{1,0:T(8,128)}), f32[64,128]{1,0:T(8,128)}) %reduce-scatter.9.cloned.1.call-update) | async-done | bytes 32784
  605.6 0.8 copy.14
  606.5 4.1 collective-permute-start.3
  610.6 0.9 collective-permute-done.3
  611.6 1.9 collective-permute-start.4
  613.5 3.1 collective-permute-done.4
  616.6 3.7 collective-permute-start.5
  620.3 1.8 scatter_custom_fusion.2
  622.2 247.9 %all-reduce.6.cloned.1.call-done = f32[64,256]{1,0:T(8,128)} async-done(((f32[64,256]{1,0:T(8,128)}), f32[64,256]{1,0:T(8,128)}) %all-reduce.6.cloned.1.call-update) | async-done | bytes 65552 | tf_op jit(solution)/shard_map/psum | solution.py:66
  870.0 1.6 gather_fusion.2
  871.7 1.3 multiply_reduce_fusion
  872.9 111.1 %psum.47 = f32[]{:T(128)} all-reduce(f32[]{:T(128)} %get-tuple-element.9), channel_id=1, replica_groups=mesh['geo'=64,'cell'=8] {'geo','cell'}, use_global_device_ids=true, to_apply=%region_14.15 | all-reduce | flops 1 | bytes 8 | tf_op jit(solution)/shard_map/psum | solution.py:92
  (46 shorter events, 7.5 us)
Async XLA Ops:
  8.0 39.5 %copy-start = (f32[64,256]{1,0:T(8,128)S(1)}, f32[64,256]{1,0:T(8,128)}, u32[]{:S(2)}) copy-start(f32[64,256]{1,0:T(8,128)} %param.15) | copy-start | bytes 196612
  9.5 32.7 %all-to-all-start = ((f32[64,2,1]{1,2,0:T(1,128)}), f32[64,2,1]{1,2,0:T(1,128)S(1)}, u32[]{:S(2)}, u32[]{:S(2)}) async-start(f32[64,2,1]{1,2,0:T(1,128)} %bitcast), calls=%async_computation | async-start | bytes 65536 | tf_op jit(solution)/shard_map/all_to_all | solution.py:40
  30.4 16.4 %copy-start.5 = (s32[128]{0:T(128)S(1)}, s32[128]{0:T(128)}, u32[]{:S(2)}) copy-start(s32[128]{0:T(128)} %param.11) | copy-start | bytes 1540
  42.1 19.8 %all-to-all-start.1 = ((f32[64,2,256]{2,1,0:T(2,128)}), f32[64,2,256]{2,1,0:T(2,128)S(1)}, u32[]{:S(2)}, u32[]{:S(2)}) async-start(f32[64,2,256]{2,1,0:T(2,128)} %all_to_all.16), calls=%async_computation.1 | async-start | bytes 262144 | tf_op jit(solution)/shard_map/all_to_all | solution.py:39
  46.8 47.7 %reduce-scatter.7.cloned.1.call-start = ((), (), s32[]{:S(2)}) async-start(), calls=%async_computation.6 | async-start | bytes 294912
  46.8 0.7 copy-start.4
  47.5 15.6 %copy-start.1 = (s32[256,512]{1,0:T(8,128)S(1)}, s32[256,512]{1,0:T(8,128)}, u32[]{:S(2)}) copy-start(s32[256,512]{1,0:T(8,128)} %param.12) | copy-start | bytes 1572868
  48.3 14.8 %copy-start.2 = (f32[128,512]{1,0:T(8,128)S(1)}, f32[128,512]{1,0:T(8,128)}, u32[]{:S(2)}) copy-start(f32[128,512]{1,0:T(8,128)} %param.14) | copy-start | bytes 786436
  62.0 1.1 copy-start.3
  65.1 293.6 %all-reduce.4.cloned.1.call-start = ((), (), s32[]{:S(2)}) async-start(), calls=%async_computation.4 | async-start | bytes 131072 | tf_op jit(solution)/shard_map/psum | solution.py:66
  95.3 5.0 collective-permute-start
  100.4 5.0 collective-permute-start.1
  105.5 254.8 %collective-permute-start.2 = (f32[256,128]{0,1:T(8,128)S(1)}, f32[256,128]{0,1:T(8,128)S(1)}, u32[]{:S(2)}, u32[]{:S(2)}) collective-permute-start(f32[256,128]{0,1:T(8,128)S(1)} %maximum_select_fusion.4), channel_id=1, source_target_pairs={{0,4},{1,5},{2,6},{3,7},{4,0},{5,1},{6,2},{7,3},{8,12},{9,13},{10,... | collective-permute-start | bytes 393224 | tf_op jit(solution)/shard_map/ppermute | solution.py:18
  111.0 494.6 %reduce-scatter.9.cloned.1.call-start = ((), (), s32[]{:S(2)}) async-start(), calls=%async_computation.7 | async-start | bytes 294912
  576.6 293.4 %all-reduce.6.cloned.1.call-start = ((), (), s32[]{:S(2)}) async-start(), calls=%async_computation.5 | async-start | bytes 131072 | tf_op jit(solution)/shard_map/psum | solution.py:66
  606.5 5.0 collective-permute-start.3
  611.6 5.0 collective-permute-start.4
  616.6 255.0 %collective-permute-start.5 = (f32[256,128]{0,1:T(8,128)S(1)}, f32[256,128]{0,1:T(8,128)S(1)}, u32[]{:S(2)}, u32[]{:S(2)}) collective-permute-start(f32[256,128]{0,1:T(8,128)S(1)} %maximum_select_fusion.5), channel_id=1, source_target_pairs={{0,4},{1,5},{2,6},{3,7},{4,0},{5,1},{6,2},{7,3},{8,12},{9,13},{10,... | collective-permute-start | bytes 393224 | tf_op jit(solution)/shard_map/ppermute | solution.py:18
Sparse Core Ops, SparseCore 0:
  65.2 29.2 reduce-scatter.6
  576.8 28.7 reduce-scatter.8
Sparse Core Ops, SparseCore 1:
  111.1 247.5 all-reduce.3
  622.3 247.7 all-reduce.5
